TPU v7x, 32 devices: a whole 2x2x4 slice. The times are simulated.
32 devices in a mesh: groups: 2 (over x), hi: 8 (over z, y), lo: 2 (over core).
Axes of the slice: x: 2, y: 2, z: 4, core: 2. Of those that a mesh axis runs over, the one named last changes fastest.
Arguments:
- vectors: float32 [64, 65536], P(None, ('groups', 'hi', 'lo')), parts along dimension 1, may hold values from -6 to 6
- tile_values: float32 [2048, 128, 128], P(('groups', 'hi', 'lo')), parts along dimension 0, may hold values from -0.25 to 0.25
- tile_cols: int32 [1024], P(('hi', 'lo')), may hold values from 0 to 15, as said below
- live_rows: int32 [16], P(('hi', 'lo')), may hold values from 512 to 2048
- boundary_map: int32 [32768], P(('hi', 'lo')), may hold values from -1 to 2047
- field_levels: int32 [8], P('groups'), parts along dimension 0, may hold values from -8 to 8
Outputs:
- filtered: float32 [64, 65536], P(None, ('groups', 'hi', 'lo')), parts along dimension 1
- correlation: float32 [128, 64], P('groups'), parts along dimension 0
- projected: float32 [128, 64], P('groups'), parts along dimension 0
There are 2 independent parts, one for each index of `groups`. A program takes and returns all parts, laid end to end along the dimension named above; an argument that names none is the same for every part. Nothing has to cross between parts.
Inputs may be any that keep to these rules, and one draw needn't show every extreme that they name: `tile_cols`: each row block's 4 column blocks are distinct.
All inputs are finite; a program needn't handle non-finite values.
Results may differ from a plain program's by a relative error of at most 0.0001.
Values sent between devices are 32-bit elements; how exact they have to be, the bound alone decides.
No kernel may reach another device: no remote copies, remote signals or barrier semaphores. Data moves between devices by JAX's collectives and lax.ppermute only.
A program may use at most 64 MiB of HBM per device.

v0:
```python
import functools

import jax
import jax.numpy as jnp
from jax import lax
from jax.experimental import pallas as pl
from jax.experimental.pallas import tpu as pltpu
from jax.sharding import PartitionSpec as P

HOP_SCALE = 0.5
ANISOTROPY = 1.0
FIELD_STEP = 0.25
HALF_WIDTH = 4.0
AXES = ("hi", "lo")
STEPS = 4
F32, BF16 = jnp.float32, jnp.bfloat16
SMEM = pl.BlockSpec(memory_space=pltpu.SMEM)
LIMIT = 32 * 1024 * 1024


def bit(number, place):
    return (number >> place) & 1


def halves(value):
    head = value.astype(BF16)
    return head, (value - head.astype(F32)).astype(BF16)


def stacked(value):
    return jnp.concatenate(halves(value), axis=0)


def product(left, right):
    rows, columns = left.shape[0] // 2, right.shape[0] // 2
    whole = lax.dot_general(left, right, (((1,), (1,)), ((), ())), preferred_element_type=F32)
    tails = whole[:rows, columns:] + whole[rows:, :columns] + whole[rows:, columns:]
    return whole[:rows, :columns] + tails


def coupling(config, bond):
    differ = bit(config, bond) ^ bit(config, bond + 1)
    return jnp.where(differ == 1, HOP_SCALE, 0.0)


def onsite_of(config, fields_ref):
    count = fields_ref.shape[0]
    spins = [bit(config, place).astype(F32) - 0.5 for place in range(count)]
    total = jnp.float32(0.0)
    for place in range(count):
        total += fields_ref[place].astype(F32) * FIELD_STEP * spins[place]
    for place in range(count - 1):
        total += ANISOTROPY * spins[place] * spins[place + 1]
    return total


def alive_of(live_ref, first, count):
    rows = lax.broadcasted_iota(jnp.int32, (1, count), 1) + first
    return (rows < live_ref[0]).astype(F32)


def own_block(block, config, cols_ref, fields_ref, field_ref, split_ref, flipped_ref, tiles_ref, map_ref):
    per_block, tile = tiles_ref.shape[1], tiles_ref.shape[2]
    span = pl.ds(pl.multiple_of(block * tile, tile), tile)
    picked = []
    for which in range(per_block):
        column = cols_ref[block * per_block + which]
        picked.append(split_ref[:, pl.ds(pl.multiple_of(column * tile, tile), tile)])
    weights = jnp.concatenate([tiles_ref[block, which] for which in range(per_block)], axis=1)
    total = product(jnp.concatenate(picked, axis=1), stacked(weights))
    total += onsite_of(config, fields_ref) * field_ref[:, span]
    targets = jnp.broadcast_to(map_ref[:, span], (8, tile))
    inside, outside = targets & (tile - 1), targets // tile
    outside = jnp.where(targets < 0, -1, outside)
    groups = []
    for group in range(field_ref.shape[0] // 8):
        found = jnp.zeros((8, tile), F32)
        for source in range(field_ref.shape[1] // tile):
            values = flipped_ref[group * 8 : group * 8 + 8, source * tile : (source + 1) * tile]
            moved = jnp.take_along_axis(values, inside, axis=1)
            found = jnp.where(outside == source, moved, found)
        groups.append(found)
    return span, total + HOP_SCALE * jnp.concatenate(groups, axis=0)


def own_kernel(place_ref, cols_ref, fields_ref, field_ref, flipped_ref, tiles_ref, map_ref, out_ref, split_ref):
    blocks = tiles_ref.shape[0] // STEPS
    split_ref[...] = stacked(field_ref[...])

    def body(step, carry):
        for row in range(blocks):
            span, total = own_block(
                step * blocks + row, place_ref[0], cols_ref, fields_ref, field_ref, split_ref, flipped_ref, tiles_ref, map_ref
            )
            out_ref[:, span] = total
        return carry

    lax.fori_loop(0, STEPS, body, 0)


def own_gram_kernel(
    place_ref, cols_ref, fields_ref, live_ref, field_ref, flipped_ref, tiles_ref, map_ref, out_ref, copy_ref, split_ref, sem
):
    blocks, tile = tiles_ref.shape[0] // STEPS, tiles_ref.shape[2]
    count, width = field_ref.shape[0], blocks * tile
    copy = pltpu.make_async_copy(field_ref, copy_ref, sem)
    copy.start()
    split_ref[...] = stacked(field_ref[...])
    out_ref[:, :count] = product(split_ref[...], split_ref[...])
    out_ref[:, count:] = jnp.zeros((count, count), F32)

    def body(step, carry):
        parts = []
        for row in range(blocks):
            block = step * blocks + row
            span, total = own_block(
                block, place_ref[0], cols_ref, fields_ref, field_ref, split_ref, flipped_ref, tiles_ref, map_ref
            )
            parts.append(alive_of(live_ref, block * tile, tile) * total)
        image = stacked(jnp.concatenate(parts, axis=1))
        span = pl.ds(pl.multiple_of(step * width, width), width)
        out_ref[:, count:] += product(split_ref[:, span], image)
        return carry

    lax.fori_loop(0, STEPS, body, 0)
    copy.wait()


def hop_sum(bonds, config, refs):
    total = coupling(config, 0) * refs[-1][...]
    total += coupling(config, 1) * jnp.concatenate([refs[-3][...], refs[-2][...]], axis=0)
    for bond, ref in zip(reversed(range(2, bonds)), refs):
        total += coupling(config, bond) * ref[...]
    return total


def store_halves(value, out_ref, first_ref, second_ref):
    middle = first_ref.shape[0]
    out_ref[...] = value
    first_ref[...] = value[:middle]
    second_ref[...] = value[middle:]


def start_kernel(live_ref, vectors_ref, out_ref, first_ref, second_ref):
    start = vectors_ref[...] * alive_of(live_ref, 0, vectors_ref.shape[1])
    store_halves(start, out_ref, first_ref, second_ref)


def combine_kernel(bonds, place_ref, live_ref, own_ref, *refs):
    hops, outs = refs[:-3], refs[-3:]
    total = own_ref[...] + hop_sum(bonds, place_ref[0], hops)
    store_halves(alive_of(live_ref, 0, total.shape[1]) * total * (1.0 / HALF_WIDTH), *outs)


def filter_kernel(bonds, place_ref, live_ref, own_ref, start_ref, *refs):
    hops, (kept_ref, sent_ref) = refs[:-2], refs[-2:]
    total = own_ref[...] + hop_sum(bonds, place_ref[0], hops)
    image = alive_of(live_ref, 0, total.shape[1]) * total * (1.0 / HALF_WIDTH)
    second = 2.0 * image - start_ref[...]
    kept_ref[...] = second
    width = sent_ref.shape[1]
    sent_ref[...] = jnp.where(place_ref[1] == 0, second[:, :width], second[:, width:])


def crossed_kernel(bonds, states, place_ref, own_ref, field_ref, *refs):
    hops, out_ref = refs[:-1], refs[-1]
    width, count = hops[-1].shape[1], own_ref.shape[0]
    near = coupling(place_ref[0], 0) * hops[-2][...] + coupling(place_ref[0], 1) * hops[-1][...]
    theirs = jnp.where(place_ref[1] == 0, 0.0, near), jnp.where(place_ref[1] == 0, near, 0.0)
    theirs = jnp.concatenate(theirs, axis=1)
    for bond, hop in zip(reversed(range(2, bonds)), hops):
        theirs += coupling(place_ref[0], bond) * hop[...]
    crossed = product(stacked(field_ref[...]), stacked(theirs))
    out_ref[:, :count] = own_ref[:, :count] * (1.0 / states)
    projected = own_ref[:, count:] + crossed + crossed.T
    out_ref[:, count:] = projected * (1.0 / (HALF_WIDTH * states))


def local(vectors, tile_values, tile_cols, live_rows, boundary_map, field_levels):
    dev_count = lax.axis_size(AXES)
    bonds = dev_count.bit_length() - 2
    flip = (dev_count - 1) // 3
    position = lax.axis_index(AXES)
    parity = sum(bit(position, place) for place in range(0, bonds + 1, 2)) & 1
    place = jnp.stack([position ^ flip, parity]).astype(jnp.int32)
    vec_count, row_count = vectors.shape
    tile_size = tile_values.shape[1]
    block_count = row_count // tile_size
    per_block = tile_values.shape[0] // block_count
    tiles = tile_values.reshape(block_count, per_block, tile_size, tile_size)
    targets = boundary_map.reshape(1, row_count)
    params = pltpu.CompilerParams(vmem_limit_bytes=LIMIT)

    def coupled(here, bond):
        return bit(here ^ flip, bond) != bit(here ^ flip, bond + 1)

    def hop(value, bond):
        pairs = [(here, here ^ (3 << bond) if coupled(here, bond) else here) for here in range(dev_count)]
        return lax.ppermute(value, AXES, pairs)

    def one_way(value, bond):
        pairs = [
            (here, here ^ (3 << bond))
            for here in range(dev_count)
            if coupled(here, bond) and bit(here, bond) != bit(here, bond - 1)
        ]
        return lax.ppermute(value, AXES, pairs)

    def near(flipped):
        pairs = [(here, here ^ (1 if coupled(here, 0) else 2)) for here in range(dev_count)]
        return lax.ppermute(flipped, AXES, pairs)

    def exchange(value, mask):
        return lax.ppermute(value, AXES, [(source, source ^ mask) for source in range(dev_count)])

    inside = pl.BlockSpec(memory_space=pltpu.VMEM)
    own_cost = pl.CostEstimate(
        flops=8 * vec_count * row_count * per_block * tile_size,
        bytes_accessed=4 * tile_values.size + 12 * vec_count * row_count,
        transcendentals=0,
    )
    split = pltpu.VMEM((2 * vec_count, row_count), BF16)
    gram_shape = jax.ShapeDtypeStruct((vec_count, 2 * vec_count), F32)

    def rows_by(count, width):
        return jax.ShapeDtypeStruct((count, width), F32)

    full = rows_by(vec_count, row_count)

    def own_part(field, flipped):
        return pl.pallas_call(
            own_kernel,
            out_shape=full,
            in_specs=[SMEM] * 3 + [inside] * 4,
            out_specs=inside,
            scratch_shapes=[split],
            compiler_params=params,
            cost_estimate=own_cost,
            name="own",
        )(place, tile_cols, field_levels, field, flipped, tiles, targets)

    def own_gram(field, flipped):
        return pl.pallas_call(
            own_gram_kernel,
            out_shape=[gram_shape, full],
            in_specs=[SMEM] * 4 + [inside] * 4,
            out_specs=[inside, pl.BlockSpec(memory_space=pl.ANY)],
            scratch_shapes=[split, pltpu.SemaphoreType.DMA(())],
            compiler_params=params,
            cost_estimate=own_cost,
            name="own_gram",
        )(place, tile_cols, field_levels, live_rows, field, flipped, tiles, targets)

    three = [full, rows_by(vec_count // 2, row_count), rows_by(vec_count // 2, row_count)]

    def apply(field, first_half, second_half):
        legs = [(here, here ^ 2) for here in range(dev_count) if coupled(here, 1)]
        round_way = [(here, here ^ 4) for here in range(dev_count) if not coupled(here, 1)]
        flipped = exchange(field, 1)
        far = [hop(field, bond) for bond in reversed(range(2, bonds))]
        aside = lax.ppermute(lax.ppermute(second_half, AXES, legs), AXES, round_way)
        direct = hop(first_half, 1)
        closest = near(flipped)
        return own_part(field, flipped), far + [direct, aside, closest]

    start, *halves_of = pl.pallas_call(
        start_kernel,
        out_shape=three,
        in_specs=[SMEM, inside],
        out_specs=[inside] * 3,
        compiler_params=params,
        name="start",
    )(live_rows, vectors)
    own, hops = apply(start, *halves_of)
    first, *halves_of = pl.pallas_call(
        functools.partial(combine_kernel, bonds),
        out_shape=three,
        in_specs=[SMEM] * 2 + [inside] * (bonds + 2),
        out_specs=[inside] * 3,
        compiler_params=params,
        name="combine",
    )(place, live_rows, own, *hops)
    own, hops = apply(first, *halves_of)
    kept, sent = pl.pallas_call(
        functools.partial(filter_kernel, bonds),
        out_shape=[full, rows_by(vec_count, row_count // 2)],
        in_specs=[SMEM] * 2 + [inside] * (bonds + 3),
        out_specs=[inside] * 2,
        compiler_params=params,
        name="filter",
    )(place, live_rows, own, start, *hops)
    flipped = exchange(kept, 1)
    hops = [one_way(kept, bond) for bond in reversed(range(2, bonds))]
    flipped, sent = lax.optimization_barrier((flipped, sent))
    hops += [hop(sent, 0), hop(sent, 1)]
    grams, second = own_gram(kept, flipped)
    sums = pl.pallas_call(
        functools.partial(crossed_kernel, bonds, dev_count * row_count),
        out_shape=gram_shape,
        in_specs=[SMEM] + [inside] * (bonds + 2),
        out_specs=inside,
        compiler_params=params,
        name="crossed",
    )(place, grams, kept, *hops)
    for digit in range(bonds + 1):
        sums = sums + exchange(sums, 1 << digit)
    return (second, sums[:, :vec_count], sums[:, vec_count:])


def solution(mesh):
    in_specs = (
        P(None, ("groups", "hi", "lo")),
        P(("groups", "hi", "lo"), None, None),
        P(("hi", "lo")),
        P(("hi", "lo")),
        P(("hi", "lo")),
        P("groups"),
    )
    out_specs = (P(None, ("groups", "hi", "lo")), P("groups", None), P("groups", None))
    return jax.shard_map(local, mesh=mesh, in_specs=in_specs, out_specs=out_specs, check_vma=False)
```

profile of v0, /device:TPU:0, one launch (start us, length us, event | category | flops | bytes accessed | tf_op | source)
XLA Modules:
  0.0 89.9 jit_solution(10883481756870131487)
XLA Ops:
  1.3 1.0 %copy-done.2 = f32[64,2048]{1,0:T(8,128)S(1)} copy-done((f32[64,2048]{1,0:T(8,128)S(1)}, f32[64,2048]{1,0:T(8,128)}, u32[]{:S(2)}) %copy-start.2) | copy-done | bytes 524312
  2.3 0.1 start.1
  2.4 0.5 collective-permute-start
  2.9 4.4 %collective-permute-start.3 = (f32[32,2048]{1,0:T(8,128)S(1)}, f32[32,2048]{1,0:T(8,128)S(1)}, u32[]{:S(2)}, u32[]{:S(2)}) collective-permute-start(f32[32,2048]{1,0:T(8,128)S(1)} %get-tuple-element.17), channel_id=1, source_target_pairs={{0,2},{1,3},{6,4},{7,5},{8,10},{9,11},{14,12},{15,13},{16,18},{17,... | collective-permute-start | bytes 786440 | tf_op jit(solution)/shard_map/ppermute | solution.py:261
  7.4 3.4 %collective-permute-start.1 = (f32[64,2048]{1,0:T(8,128)S(1)}, f32[64,2048]{1,0:T(8,128)S(1)}, u32[]{:S(2)}, u32[]{:S(2)}) collective-permute-start(f32[64,2048]{1,0:T(8,128)S(1)} %get-tuple-element.15.field_ref.start_ref), channel_id=1, source_target_pairs={{0,12},{1,13},{2,14},{3,15},{4,4},{5,5},{6,6},{7,7},{8,8},{9,9},{1... | collective-permute-start | bytes 1572872 | tf_op jit(solution)/shard_map/ppermute | solution.py:199
  10.8 0.2 collective-permute-start.5
  11.0 1.9 %collective-permute-start.2 = (f32[32,2048]{1,0:T(8,128)S(1)}, f32[32,2048]{1,0:T(8,128)S(1)}, u32[]{:S(2)}, u32[]{:S(2)}) collective-permute-start(f32[32,2048]{1,0:T(8,128)S(1)} %get-tuple-element.16), channel_id=1, source_target_pairs={{0,6},{1,7},{2,2},{3,3},{4,4},{5,5},{6,0},{7,1},{8,14},{9,15},{10,... | collective-permute-start | bytes 786440 | tf_op jit(solution)/shard_map/ppermute | solution.py:199
  12.9 0.7 collective-permute-done.3
  13.6 1.3 %collective-permute-start.4 = (f32[32,2048]{1,0:T(8,128)S(1)}, f32[32,2048]{1,0:T(8,128)S(1)}, u32[]{:S(2)}, u32[]{:S(2)}) collective-permute-start(f32[32,2048]{1,0:T(8,128)S(1)} %collective-permute-done.3), channel_id=1, source_target_pairs={{2,6},{3,7},{4,0},{5,1},{10,14},{11,15},{12,8},{13,9},{18,22},{19,... | collective-permute-start | bytes 786440 | tf_op jit(solution)/shard_map/ppermute | solution.py:261
  14.8 0.1 pad_add_fusion.place_ref
  14.9 2.2 %copy-done = f32[64,128,128]{2,1,0:T(8,128)S(1)} copy-done((f32[64,128,128]{2,1,0:T(8,128)S(1)}, f32[64,128,128]{2,1,0:T(8,128)}, u32[]{:S(2)}) %copy-start) | copy-done | bytes 4194328
  17.1 0.7 copy-done.3
  17.8 0.7 copy-done.5
  18.5 0.7 copy-done.6
  19.1 3.6 %own.2.own_ref = f32[64,2048]{1,0:T(8,128)S(1)} custom-call(s32[2]{0:T(128)S(1)} %pad_add_fusion.place_ref, s32[64]{0:T(128)S(1)} %copy-done.5, s32[4]{0:T(128)S(1)} %copy-done.6, f32[64,2048]{1,0:T(8,128)S(1)} %get-tuple-element.15.field_ref.start_ref, f32[64,2048]{1,0:T(8,128)S(1)} %collective-permute-done.flipped_ref, f32[16,4,128,128]{3,2,1,0:T(8,128)S(1)} %bitcast.4, ...), custom_call_target="tpu_custom_call" | custom-call | flops 536870912 | bytes 5767168 | tf_op jit(solution)/shard_map/own/pallas_call | solution.py:231
  22.7 7.9 %collective-permute-done.2.refs_1_ = f32[32,2048]{1,0:T(8,128)S(1)} collective-permute-done((f32[32,2048]{1,0:T(8,128)S(1)}, f32[32,2048]{1,0:T(8,128)S(1)}, u32[]{:S(2)}, u32[]{:S(2)}) %collective-permute-start.2) | collective-permute-done | bytes 262176 | tf_op jit(solution)/shard_map/ppermute | solution.py:199
  30.6 0.0 collective-permute-done.4.refs_2_
  30.7 0.0 collective-permute-done.1.refs_0_
  30.7 0.0 collective-permute-done.5.refs_3_
  30.7 0.7 combine.1
  31.4 0.2 collective-permute-start.6
  31.6 1.9 %collective-permute-start.7 = (f32[64,2048]{1,0:T(8,128)S(1)}, f32[64,2048]{1,0:T(8,128)S(1)}, u32[]{:S(2)}, u32[]{:S(2)}) collective-permute-start(f32[64,2048]{1,0:T(8,128)S(1)} %get-tuple-element.18.field_ref), channel_id=1, source_target_pairs={{0,12},{1,13},{2,14},{3,15},{4,4},{5,5},{6,6},{7,7},{8,8},{9,9},{1... | collective-permute-start | bytes 1572872 | tf_op jit(solution)/shard_map/ppermute | solution.py:199
  33.5 6.0 %collective-permute-start.9 = (f32[32,2048]{1,0:T(8,128)S(1)}, f32[32,2048]{1,0:T(8,128)S(1)}, u32[]{:S(2)}, u32[]{:S(2)}) collective-permute-start(f32[32,2048]{1,0:T(8,128)S(1)} %get-tuple-element.20), channel_id=1, source_target_pairs={{0,2},{1,3},{6,4},{7,5},{8,10},{9,11},{14,12},{15,13},{16,18},{17,... | collective-permute-start | bytes 786440 | tf_op jit(solution)/shard_map/ppermute | solution.py:261
  39.5 0.0 collective-permute-done.6.flipped_ref
  39.5 0.0 collective-permute-start.11
  39.5 0.0 copy-start.4
  39.5 1.9 %collective-permute-start.8 = (f32[32,2048]{1,0:T(8,128)S(1)}, f32[32,2048]{1,0:T(8,128)S(1)}, u32[]{:S(2)}, u32[]{:S(2)}) collective-permute-start(f32[32,2048]{1,0:T(8,128)S(1)} %get-tuple-element.19), channel_id=1, source_target_pairs={{0,6},{1,7},{2,2},{3,3},{4,4},{5,5},{6,0},{7,1},{8,14},{9,15},{10,... | collective-permute-start | bytes 786440 | tf_op jit(solution)/shard_map/ppermute | solution.py:199
  41.4 4.6 %collective-permute-done.9 = f32[32,2048]{1,0:T(8,128)S(1)} collective-permute-done((f32[32,2048]{1,0:T(8,128)S(1)}, f32[32,2048]{1,0:T(8,128)S(1)}, u32[]{:S(2)}, u32[]{:S(2)}) %collective-permute-start.9) | collective-permute-done | bytes 262176 | tf_op jit(solution)/shard_map/ppermute | solution.py:261
  46.1 1.3 %collective-permute-start.10 = (f32[32,2048]{1,0:T(8,128)S(1)}, f32[32,2048]{1,0:T(8,128)S(1)}, u32[]{:S(2)}, u32[]{:S(2)}) collective-permute-start(f32[32,2048]{1,0:T(8,128)S(1)} %collective-permute-done.9), channel_id=1, source_target_pairs={{2,6},{3,7},{4,0},{5,1},{10,14},{11,15},{12,8},{13,9},{18,22},{19,... | collective-permute-start | bytes 786440 | tf_op jit(solution)/shard_map/ppermute | solution.py:261
  47.4 3.6 %own.3.own_ref = f32[64,2048]{1,0:T(8,128)S(1)} custom-call(s32[2]{0:T(128)S(1)} %pad_add_fusion.place_ref, s32[64]{0:T(128)S(1)} %copy-done.5, s32[4]{0:T(128)S(1)} %copy-done.6, f32[64,2048]{1,0:T(8,128)S(1)} %get-tuple-element.18.field_ref, f32[64,2048]{1,0:T(8,128)S(1)} %collective-permute-done.6.flipped_ref, f32[16,4,128,128]{3,2,1,0:T(8,128)S(1)} %bitcast.5, ...), custom_call_target="tpu_custom_call" | custom-call | flops 536870912 | bytes 5767168 | tf_op jit(solution)/shard_map/own/pallas_call | solution.py:231
  51.0 4.1 %collective-permute-done.8.refs_1_ = f32[32,2048]{1,0:T(8,128)S(1)} collective-permute-done((f32[32,2048]{1,0:T(8,128)S(1)}, f32[32,2048]{1,0:T(8,128)S(1)}, u32[]{:S(2)}, u32[]{:S(2)}) %collective-permute-start.8) | collective-permute-done | bytes 262176 | tf_op jit(solution)/shard_map/ppermute | solution.py:199
  55.1 0.1 collective-permute-done.10.refs_2_
  55.2 0.8 filter.1
  56.0 0.1 collective-permute-start.12
  56.1 1.3 %collective-permute-start.13 = (f32[64,2048]{1,0:T(8,128)S(1)}, f32[64,2048]{1,0:T(8,128)S(1)}, u32[]{:S(2)}, u32[]{:S(2)}) collective-permute-start(f32[64,2048]{1,0:T(8,128)S(1)} %get-tuple-element.21.field_ref), channel_id=1, source_target_pairs={{2,14},{3,15},{12,0},{13,1},{18,30},{19,31},{28,16},{29,17}} | collective-permute-start | bytes 1572872 | tf_op jit(solution)/shard_map/ppermute | solution.py:207
  57.4 0.6 collective-permute-done.12.flipped_ref
  58.0 3.5 %collective-permute-start.15 = (f32[64,1024]{1,0:T(8,128)S(1)}, f32[64,1024]{1,0:T(8,128)S(1)}, u32[]{:S(2)}, u32[]{:S(2)}) collective-permute-start(f32[64,1024]{1,0:T(8,128)S(1)} %get-tuple-element.26), channel_id=1, source_target_pairs={{0,6},{1,7},{2,2},{3,3},{4,4},{5,5},{6,0},{7,1},{8,14},{9,15},{10,... | collective-permute-start | bytes 786440 | tf_op jit(solution)/shard_map/ppermute | solution.py:199
  61.5 2.9 %collective-permute-start.14 = (f32[64,1024]{1,0:T(8,128)S(1)}, f32[64,1024]{1,0:T(8,128)S(1)}, u32[]{:S(2)}, u32[]{:S(2)}) collective-permute-start(f32[64,1024]{1,0:T(8,128)S(1)} %get-tuple-element.26), channel_id=1, source_target_pairs={{0,3},{1,1},{2,2},{3,0},{4,7},{5,5},{6,6},{7,4},{8,11},{9,9},{10,1... | collective-permute-start | bytes 786440 | tf_op jit(solution)/shard_map/ppermute | solution.py:199
  64.5 5.7 %own_gram.1 = (f32[64,128]{1,0:T(8,128)S(1)}, f32[64,2048]{1,0:T(8,128)}) custom-call(s32[2]{0:T(128)S(1)} %pad_add_fusion.place_ref, s32[64]{0:T(128)S(1)} %copy-done.5, s32[4]{0:T(128)S(1)} %copy-done.6, s32[1]{0:T(128)S(6)} %copy.9.live_ref, f32[64,2048]{1,0:T(8,128)S(1)} %get-tuple-element.21.field_ref, ...), custom_call_target="tpu_custom_call" | custom-call | flops 536870912 | bytes 5767168 | tf_op jit(solution)/shard_map/own_gram/pallas_call | solution.py:243
  70.2 3.9 %collective-permute-done.13.refs_0_ = f32[64,2048]{1,0:T(8,128)S(1)} collective-permute-done((f32[64,2048]{1,0:T(8,128)S(1)}, f32[64,2048]{1,0:T(8,128)S(1)}, u32[]{:S(2)}, u32[]{:S(2)}) %collective-permute-start.13) | collective-permute-done | bytes 524320 | tf_op jit(solution)/shard_map/ppermute | solution.py:207
  74.1 1.2 %crossed.1 = f32[64,128]{1,0:T(8,128)S(1)} custom-call(s32[2]{0:T(128)S(1)} %pad_add_fusion.place_ref, f32[64,128]{1,0:T(8,128)S(1)} %get-tuple-element.25.own_ref, f32[64,2048]{1,0:T(8,128)S(1)} %get-tuple-element.21.field_ref, f32[64,2048]{1,0:T(8,128)S(1)} %collective-permute-done.13.refs_0_, f32[64,1024]{1,0:T(8,128)S(1)} %collective-permute-done.14.refs_1_, ...), custom_call_target="tpu_custom_call" | custom-call | tf_op jit(solution)/shard_map/crossed/pallas_call | solution.py:297
  75.3 0.1 collective-permute-start.16
  75.4 1.2 %collective-permute-done.16 = f32[64,128]{1,0:T(8,128)S(1)} collective-permute-done((f32[64,128]{1,0:T(8,128)S(1)}, f32[64,128]{1,0:T(8,128)S(1)}, u32[]{:S(2)}, u32[]{:S(2)}) %collective-permute-start.16) | collective-permute-done | bytes 32800 | tf_op jit(solution)/shard_map/ppermute | solution.py:214
  76.6 3.9 %collective-permute-done.17 = f32[64,128]{1,0:T(8,128)S(1)} collective-permute-done((f32[64,128]{1,0:T(8,128)S(1)}, f32[64,128]{1,0:T(8,128)S(1)}, u32[]{:S(2)}, u32[]{:S(2)}) %collective-permute-start.17) | collective-permute-done | bytes 32800 | tf_op jit(solution)/shard_map/ppermute | solution.py:214
  80.5 3.9 %collective-permute-done.18 = f32[64,128]{1,0:T(8,128)S(1)} collective-permute-done((f32[64,128]{1,0:T(8,128)S(1)}, f32[64,128]{1,0:T(8,128)S(1)}, u32[]{:S(2)}, u32[]{:S(2)}) %collective-permute-start.18) | collective-permute-done | bytes 32800 | tf_op jit(solution)/shard_map/ppermute | solution.py:214
  84.4 0.5 collective-permute-start.19
  84.9 4.3 %collective-permute-done.19 = f32[64,128]{1,0:T(8,128)S(1)} collective-permute-done((f32[64,128]{1,0:T(8,128)S(1)}, f32[64,128]{1,0:T(8,128)S(1)}, u32[]{:S(2)}, u32[]{:S(2)}) %collective-permute-start.19) | collective-permute-done | bytes 32800 | tf_op jit(solution)/shard_map/ppermute | solution.py:214
  89.2 0.7 fusion
  (19 shorter events, 0.1 us)
Async XLA Ops:
  1.3 1.0 %copy-start.2 = (f32[64,2048]{1,0:T(8,128)S(1)}, f32[64,2048]{1,0:T(8,128)}, u32[]{:S(2)}) copy-start(f32[64,2048]{1,0:T(8,128)} %vectors_ref.1) | copy-start | bytes 1572868
  2.4 8.3 %collective-permute-start = (f32[64,2048]{1,0:T(8,128)S(1)}, f32[64,2048]{1,0:T(8,128)S(1)}, u32[]{:S(2)}, u32[]{:S(2)}) collective-permute-start(f32[64,2048]{1,0:T(8,128)S(1)} %get-tuple-element.15.field_ref.start_ref), channel_id=1, source_target_pairs={{0,1},{1,0},{2,3},{3,2},{4,5},{5,4},{6,7},{7,6},{8,9},{9,8},{10,11... | collective-permute-start | bytes 1572872 | tf_op jit(solution)/shard_map/ppermute | solution.py:214
  2.9 10.6 %collective-permute-start.3 = (f32[32,2048]{1,0:T(8,128)S(1)}, f32[32,2048]{1,0:T(8,128)S(1)}, u32[]{:S(2)}, u32[]{:S(2)}) collective-permute-start(f32[32,2048]{1,0:T(8,128)S(1)} %get-tuple-element.17), channel_id=1, source_target_pairs={{0,2},{1,3},{6,4},{7,5},{8,10},{9,11},{14,12},{15,13},{16,18},{17,... | collective-permute-start | bytes 786440 | tf_op jit(solution)/shard_map/ppermute | solution.py:261
  7.4 23.3 %collective-permute-start.1 = (f32[64,2048]{1,0:T(8,128)S(1)}, f32[64,2048]{1,0:T(8,128)S(1)}, u32[]{:S(2)}, u32[]{:S(2)}) collective-permute-start(f32[64,2048]{1,0:T(8,128)S(1)} %get-tuple-element.15.field_ref.start_ref), channel_id=1, source_target_pairs={{0,12},{1,13},{2,14},{3,15},{4,4},{5,5},{6,6},{7,7},{8,8},{9,9},{1... | collective-permute-start | bytes 1572872 | tf_op jit(solution)/shard_map/ppermute | solution.py:199
  10.8 19.9 %collective-permute-start.5 = (f32[64,2048]{1,0:T(8,128)S(1)}, f32[64,2048]{1,0:T(8,128)S(1)}, u32[]{:S(2)}, u32[]{:S(2)}) collective-permute-start(f32[64,2048]{1,0:T(8,128)S(1)} %collective-permute-done.flipped_ref), channel_id=1, source_target_pairs={{0,1},{1,3},{2,0},{3,2},{4,5},{5,7},{6,4},{7,6},{8,9},{9,11},{10,8... | collective-permute-start | bytes 1572872 | tf_op jit(solution)/shard_map/ppermute | solution.py:211
  11.0 19.7 %collective-permute-start.2 = (f32[32,2048]{1,0:T(8,128)S(1)}, f32[32,2048]{1,0:T(8,128)S(1)}, u32[]{:S(2)}, u32[]{:S(2)}) collective-permute-start(f32[32,2048]{1,0:T(8,128)S(1)} %get-tuple-element.16), channel_id=1, source_target_pairs={{0,6},{1,7},{2,2},{3,3},{4,4},{5,5},{6,0},{7,1},{8,14},{9,15},{10,... | collective-permute-start | bytes 786440 | tf_op jit(solution)/shard_map/ppermute | solution.py:199
  13.6 17.1 %collective-permute-start.4 = (f32[32,2048]{1,0:T(8,128)S(1)}, f32[32,2048]{1,0:T(8,128)S(1)}, u32[]{:S(2)}, u32[]{:S(2)}) collective-permute-start(f32[32,2048]{1,0:T(8,128)S(1)} %collective-permute-done.3), channel_id=1, source_target_pairs={{2,6},{3,7},{4,0},{5,1},{10,14},{11,15},{12,8},{13,9},{18,22},{19,... | collective-permute-start | bytes 786440 | tf_op jit(solution)/shard_map/ppermute | solution.py:261
  14.9 2.2 %copy-start = (f32[64,128,128]{2,1,0:T(8,128)S(1)}, f32[64,128,128]{2,1,0:T(8,128)}, u32[]{:S(2)}) copy-start(f32[64,128,128]{2,1,0:T(8,128)} %param.7) | copy-start | bytes 12582916
  17.1 0.7 copy-start.3
  17.8 0.7 copy-start.5
  18.5 0.7 copy-start.6
  19.1 28.3 %copy-start.1 = (f32[64,128,128]{2,1,0:T(8,128)S(1)}, f32[64,128,128]{2,1,0:T(8,128)}, u32[]{:S(2)}) copy-start(f32[64,128,128]{2,1,0:T(8,128)} %param.7) | copy-start | bytes 12582916
  31.4 8.1 %collective-permute-start.6 = (f32[64,2048]{1,0:T(8,128)S(1)}, f32[64,2048]{1,0:T(8,128)S(1)}, u32[]{:S(2)}, u32[]{:S(2)}) collective-permute-start(f32[64,2048]{1,0:T(8,128)S(1)} %get-tuple-element.18.field_ref), channel_id=1, source_target_pairs={{0,1},{1,0},{2,3},{3,2},{4,5},{5,4},{6,7},{7,6},{8,9},{9,8},{10,11... | collective-permute-start | bytes 1572872 | tf_op jit(solution)/shard_map/ppermute | solution.py:214
  31.6 23.6 %collective-permute-start.7 = (f32[64,2048]{1,0:T(8,128)S(1)}, f32[64,2048]{1,0:T(8,128)S(1)}, u32[]{:S(2)}, u32[]{:S(2)}) collective-permute-start(f32[64,2048]{1,0:T(8,128)S(1)} %get-tuple-element.18.field_ref), channel_id=1, source_target_pairs={{0,12},{1,13},{2,14},{3,15},{4,4},{5,5},{6,6},{7,7},{8,8},{9,9},{1... | collective-permute-start | bytes 1572872 | tf_op jit(solution)/shard_map/ppermute | solution.py:199
  33.5 12.6 %collective-permute-start.9 = (f32[32,2048]{1,0:T(8,128)S(1)}, f32[32,2048]{1,0:T(8,128)S(1)}, u32[]{:S(2)}, u32[]{:S(2)}) collective-permute-start(f32[32,2048]{1,0:T(8,128)S(1)} %get-tuple-element.20), channel_id=1, source_target_pairs={{0,2},{1,3},{6,4},{7,5},{8,10},{9,11},{14,12},{15,13},{16,18},{17,... | collective-permute-start | bytes 786440 | tf_op jit(solution)/shard_map/ppermute | solution.py:261
  39.5 15.8 %collective-permute-start.11 = (f32[64,2048]{1,0:T(8,128)S(1)}, f32[64,2048]{1,0:T(8,128)S(1)}, u32[]{:S(2)}, u32[]{:S(2)}) collective-permute-start(f32[64,2048]{1,0:T(8,128)S(1)} %collective-permute-done.6.flipped_ref), channel_id=1, source_target_pairs={{0,1},{1,3},{2,0},{3,2},{4,5},{5,7},{6,4},{7,6},{8,9},{9,11},{10,8... | collective-permute-start | bytes 1572872 | tf_op jit(solution)/shard_map/ppermute | solution.py:211
  39.5 25.0 %copy-start.4 = (s32[2048]{0:T(1024)S(1)}, s32[2048]{0:T(1024)}, u32[]{:S(2)}) copy-start(s32[2048]{0:T(1024)} %param.10) | copy-start | bytes 24580
  39.5 15.6 %collective-permute-start.8 = (f32[32,2048]{1,0:T(8,128)S(1)}, f32[32,2048]{1,0:T(8,128)S(1)}, u32[]{:S(2)}, u32[]{:S(2)}) collective-permute-start(f32[32,2048]{1,0:T(8,128)S(1)} %get-tuple-element.19), channel_id=1, source_target_pairs={{0,6},{1,7},{2,2},{3,3},{4,4},{5,5},{6,0},{7,1},{8,14},{9,15},{10,... | collective-permute-start | bytes 786440 | tf_op jit(solution)/shard_map/ppermute | solution.py:199
  46.1 9.1 %collective-permute-start.10 = (f32[32,2048]{1,0:T(8,128)S(1)}, f32[32,2048]{1,0:T(8,128)S(1)}, u32[]{:S(2)}, u32[]{:S(2)}) collective-permute-start(f32[32,2048]{1,0:T(8,128)S(1)} %collective-permute-done.9), channel_id=1, source_target_pairs={{2,6},{3,7},{4,0},{5,1},{10,14},{11,15},{12,8},{13,9},{18,22},{19,... | collective-permute-start | bytes 786440 | tf_op jit(solution)/shard_map/ppermute | solution.py:261
  56.0 2.0 %collective-permute-start.12 = (f32[64,2048]{1,0:T(8,128)S(1)}, f32[64,2048]{1,0:T(8,128)S(1)}, u32[]{:S(2)}, u32[]{:S(2)}) collective-permute-start(f32[64,2048]{1,0:T(8,128)S(1)} %get-tuple-element.21.field_ref), channel_id=1, source_target_pairs={{0,1},{1,0},{2,3},{3,2},{4,5},{5,4},{6,7},{7,6},{8,9},{9,8},{10,11... | collective-permute-start | bytes 1572872 | tf_op jit(solution)/shard_map/ppermute | solution.py:214
  56.1 18.0 %collective-permute-start.13 = (f32[64,2048]{1,0:T(8,128)S(1)}, f32[64,2048]{1,0:T(8,128)S(1)}, u32[]{:S(2)}, u32[]{:S(2)}) collective-permute-start(f32[64,2048]{1,0:T(8,128)S(1)} %get-tuple-element.21.field_ref), channel_id=1, source_target_pairs={{2,14},{3,15},{12,0},{13,1},{18,30},{19,31},{28,16},{29,17}} | collective-permute-start | bytes 1572872 | tf_op jit(solution)/shard_map/ppermute | solution.py:207
  58.0 16.1 %collective-permute-start.15 = (f32[64,1024]{1,0:T(8,128)S(1)}, f32[64,1024]{1,0:T(8,128)S(1)}, u32[]{:S(2)}, u32[]{:S(2)}) collective-permute-start(f32[64,1024]{1,0:T(8,128)S(1)} %get-tuple-element.26), channel_id=1, source_target_pairs={{0,6},{1,7},{2,2},{3,3},{4,4},{5,5},{6,0},{7,1},{8,14},{9,15},{10,... | collective-permute-start | bytes 786440 | tf_op jit(solution)/shard_map/ppermute | solution.py:199
  61.5 12.6 %collective-permute-start.14 = (f32[64,1024]{1,0:T(8,128)S(1)}, f32[64,1024]{1,0:T(8,128)S(1)}, u32[]{:S(2)}, u32[]{:S(2)}) collective-permute-start(f32[64,1024]{1,0:T(8,128)S(1)} %get-tuple-element.26), channel_id=1, source_target_pairs={{0,3},{1,1},{2,2},{3,0},{4,7},{5,5},{6,6},{7,4},{8,11},{9,9},{10,1... | collective-permute-start | bytes 786440 | tf_op jit(solution)/shard_map/ppermute | solution.py:199
  75.3 1.3 %collective-permute-start.16 = (f32[64,128]{1,0:T(8,128)S(1)}, f32[64,128]{1,0:T(8,128)S(1)}, u32[]{:S(2)}, u32[]{:S(2)}) collective-permute-start(f32[64,128]{1,0:T(8,128)S(1)} %crossed.1), channel_id=1, source_target_pairs={{0,1},{1,0},{2,3},{3,2},{4,5},{5,4},{6,7},{7,6},{8,9},{9,8},{10,11... | collective-permute-start | bytes 98312 | tf_op jit(solution)/shard_map/ppermute | solution.py:214
  76.6 3.9 %collective-permute-start.17 = (f32[64,128]{1,0:T(8,128)S(1)}, f32[64,128]{1,0:T(8,128)S(1)}, u32[]{:S(2)}, u32[]{:S(2)}) collective-permute-start(f32[64,128]{1,0:T(8,128)S(1)} %add.20), channel_id=1, source_target_pairs={{0,2},{1,3},{2,0},{3,1},{4,6},{5,7},{6,4},{7,5},{8,10},{9,11},{10,... | collective-permute-start | bytes 98312 | tf_op jit(solution)/shard_map/ppermute | solution.py:214
  80.5 3.9 %collective-permute-start.18 = (f32[64,128]{1,0:T(8,128)S(1)}, f32[64,128]{1,0:T(8,128)S(1)}, u32[]{:S(2)}, u32[]{:S(2)}) collective-permute-start(f32[64,128]{1,0:T(8,128)S(1)} %add.21), channel_id=1, source_target_pairs={{0,4},{1,5},{2,6},{3,7},{4,0},{5,1},{6,2},{7,3},{8,12},{9,13},{10,... | collective-permute-start | bytes 98312 | tf_op jit(solution)/shard_map/ppermute | solution.py:214
  84.4 4.8 %collective-permute-start.19 = (f32[64,128]{1,0:T(8,128)S(1)}, f32[64,128]{1,0:T(8,128)S(1)}, u32[]{:S(2)}, u32[]{:S(2)}) collective-permute-start(f32[64,128]{1,0:T(8,128)S(1)} %add.22), channel_id=1, source_target_pairs={{0,8},{1,9},{2,10},{3,11},{4,12},{5,13},{6,14},{7,15},{8,0},{9,1},... | collective-permute-start | bytes 98312 | tf_op jit(solution)/shard_map/ppermute | solution.py:214
where the time goes:
time: 90.5 us; the launch traced here: 89.9 us
  waiting for transfers between devices  35.3 us (39%)
  starting transfers between devices  31.4 us (35%)
  Pallas kernels  15.7 us (17%)
  local copies, waits for them, and re-layouts  5.93 us (7%)
  between operations  1.52 us (2%)
    ppermute x6, starting transfers between devices, hop(): return lax.ppermute(value, AXES, pairs)  15.6 us
    ppermute x7, waiting for transfers between devices, exchange(): lax.ppermute(value, AXES, [(source, source ^ mask) for source in range(de...  13.9 us
    ppermute x4, starting transfers between devices, apply(): aside = lax.ppermute(lax.ppermute(second_half, AXES, legs), AXES, round_way)  13 us
    ppermute x6, waiting for transfers between devices, hop(): return lax.ppermute(value, AXES, pairs)  12 us
    pallas_call x2, Pallas kernels, own_part(): pl.pallas_call(own_kernel, out_shape=full, in_specs=[SMEM] * 3 + [inside]...  7.22 us
    pallas_call x1, Pallas kernels, own_gram(): pl.pallas_call(own_gram_kernel, out_shape=[gram_shape, full], in_specs=[S...  5.71 us
    ppermute x4, waiting for transfers between devices, apply(): aside = lax.ppermute(lax.ppermute(second_half, AXES, legs), AXES, round_way)  5.44 us
    unnamed x14, local copies, waits for them, and re-layouts  5.24 us
  transfers between devices with their start and end apart: 20, of which 11 were waited for; matrix products, arithmetic and copies ran while one was open for 0% of the time, Pallas kernels for 14%

commit v1 on v0

--- a/solution.py
+++ b/solution.py
@@ -153,11 +153,13 @@
 
 
 def filter_kernel(bonds, place_ref, live_ref, own_ref, start_ref, *refs):
-    hops, (kept_ref, sent_ref) = refs[:-2], refs[-2:]
+    hops, (kept_ref, sent_ref, lead_ref, rest_ref) = refs[:-4], refs[-4:]
     total = own_ref[...] + hop_sum(bonds, place_ref[0], hops)
     image = alive_of(live_ref, 0, total.shape[1]) * total * (1.0 / HALF_WIDTH)
     second = 2.0 * image - start_ref[...]
     kept_ref[...] = second
+    lead_ref[...] = second[:, : lead_ref.shape[1]]
+    rest_ref[...] = second[:, lead_ref.shape[1] :]
     width = sent_ref.shape[1]
     sent_ref[...] = jnp.where(place_ref[1] == 0, second[:, :width], second[:, width:])
 
@@ -168,8 +170,8 @@
     near = coupling(place_ref[0], 0) * hops[-2][...] + coupling(place_ref[0], 1) * hops[-1][...]
     theirs = jnp.where(place_ref[1] == 0, 0.0, near), jnp.where(place_ref[1] == 0, near, 0.0)
     theirs = jnp.concatenate(theirs, axis=1)
-    for bond, hop in zip(reversed(range(2, bonds)), hops):
-        theirs += coupling(place_ref[0], bond) * hop[...]
+    for bond, lead, rest in zip(reversed(range(2, bonds)), hops, hops[bonds - 2 :]):
+        theirs += coupling(place_ref[0], bond) * jnp.concatenate([lead[...], rest[...]], axis=1)
     crossed = product(stacked(field_ref[...]), stacked(theirs))
     out_ref[:, :count] = own_ref[:, :count] * (1.0 / states)
     projected = own_ref[:, count:] + crossed + crossed.T
@@ -198,11 +200,11 @@
         pairs = [(here, here ^ (3 << bond) if coupled(here, bond) else here) for here in range(dev_count)]
         return lax.ppermute(value, AXES, pairs)
 
-    def one_way(value, bond):
+    def one_way(value, bond, lead):
         pairs = [
             (here, here ^ (3 << bond))
             for here in range(dev_count)
-            if coupled(here, bond) and bit(here, bond) != bit(here, bond - 1)
+            if coupled(here, bond) and bit(here, bond) ^ bit(here, bond - 1) == lead
         ]
         return lax.ppermute(value, AXES, pairs)
 
@@ -281,23 +283,25 @@
         name="combine",
     )(place, live_rows, own, *hops)
     own, hops = apply(first, *halves_of)
-    kept, sent = pl.pallas_call(
+    cut = row_count * 3 // 4
+    kept, sent, lead, rest = pl.pallas_call(
         functools.partial(filter_kernel, bonds),
-        out_shape=[full, rows_by(vec_count, row_count // 2)],
+        out_shape=[full] + [rows_by(vec_count, width) for width in (row_count // 2, cut, row_count - cut)],
         in_specs=[SMEM] * 2 + [inside] * (bonds + 3),
-        out_specs=[inside] * 2,
+        out_specs=[inside] * 4,
         compiler_params=params,
         name="filter",
     )(place, live_rows, own, start, *hops)
     flipped = exchange(kept, 1)
-    hops = [one_way(kept, bond) for bond in reversed(range(2, bonds))]
-    flipped, sent = lax.optimization_barrier((flipped, sent))
+    hops = [one_way(lead, bond, 1) for bond in reversed(range(2, bonds))]
+    flipped, sent, rest = lax.optimization_barrier((flipped, sent, rest))
+    hops += [one_way(rest, bond, 0) for bond in reversed(range(2, bonds))]
     hops += [hop(sent, 0), hop(sent, 1)]
     grams, second = own_gram(kept, flipped)
     sums = pl.pallas_call(
         functools.partial(crossed_kernel, bonds, dev_count * row_count),
         out_shape=gram_shape,
-        in_specs=[SMEM] + [inside] * (bonds + 2),
+        in_specs=[SMEM] + [inside] * (2 * bonds),
         out_specs=inside,
         compiler_params=params,
         name="crossed",

time: 90.5 us -> 89.6 us (0.990)
  waiting for transfers between devices: 35.3 us -> 31.9 us
  starting transfers between devices: 31.4 us -> 34 us
    ppermute x1 -> x2, waiting for transfers between devices: 3.91 us -> 0.01 us  [one_way(): return lax.ppermute(value, AXES, pairs)]
    ppermute x1 -> x2, starting transfers between devices: 1.29 us -> 4.32 us  [one_way(): return lax.ppermute(value, AXES, pairs)]
    unnamed x14 -> x12, local copies, waits for them, and re-layouts: 5.24 us -> 5.23 us
  transfers between devices with their start and end apart: 20 -> 21, of which waited for: 11 -> 10; matrix products, arithmetic and copies ran while one was open for 0% -> 0% of each run, Pallas kernels for 14% -> 15%
where the time goes in v1:
time: 89.6 us; the launch traced here: 89.1 us
  starting transfers between devices  34 us (38%)
  waiting for transfers between devices  31.9 us (36%)
  Pallas kernels  15.7 us (18%)
  local copies, waits for them, and re-layouts  5.93 us (7%)
  between operations  1.54 us (2%)
    ppermute x6, starting transfers between devices, hop(): return lax.ppermute(value, AXES, pairs)  15.5 us
    ppermute x7, waiting for transfers between devices, exchange(): lax.ppermute(value, AXES, [(source, source ^ mask) for source in range(de...  14.4 us
    ppermute x4, starting transfers between devices, apply(): aside = lax.ppermute(lax.ppermute(second_half, AXES, legs), AXES, round_way)  13 us
    ppermute x6, waiting for transfers between devices, hop(): return lax.ppermute(value, AXES, pairs)  12 us
    pallas_call x2, Pallas kernels, own_part(): pl.pallas_call(own_kernel, out_shape=full, in_specs=[SMEM] * 3 + [inside]...  7.23 us
    pallas_call x1, Pallas kernels, own_gram(): pl.pallas_call(own_gram_kernel, out_shape=[gram_shape, full], in_specs=[S...  5.71 us
    ppermute x4, waiting for transfers between devices, apply(): aside = lax.ppermute(lax.ppermute(second_half, AXES, legs), AXES, round_way)  5.45 us
    unnamed x12, local copies, waits for them, and re-layouts  5.23 us
  transfers between devices with their start and end apart: 21, of which 10 were waited for; matrix products, arithmetic and copies ran while one was open for 0% of the time, Pallas kernels for 15%

profile of v1, /device:TPU:0, one launch (start us, length us, event | category | flops | bytes accessed | tf_op | source)
XLA Modules:
  0.0 89.1 jit_solution(938714384486123722)
XLA Ops:
  1.3 1.0 %copy-done.2 = f32[64,2048]{1,0:T(8,128)S(1)} copy-done((f32[64,2048]{1,0:T(8,128)S(1)}, f32[64,2048]{1,0:T(8,128)}, u32[]{:S(2)}) %copy-start.2) | copy-done | bytes 524312
  2.3 0.1 start.1
  2.4 0.5 collective-permute-start
  2.9 4.4 %collective-permute-start.3 = (f32[32,2048]{1,0:T(8,128)S(1)}, f32[32,2048]{1,0:T(8,128)S(1)}, u32[]{:S(2)}, u32[]{:S(2)}) collective-permute-start(f32[32,2048]{1,0:T(8,128)S(1)} %get-tuple-element.20), channel_id=1, source_target_pairs={{0,2},{1,3},{6,4},{7,5},{8,10},{9,11},{14,12},{15,13},{16,18},{17,... | collective-permute-start | bytes 786440 | tf_op jit(solution)/shard_map/ppermute | solution.py:263
  7.4 3.4 %collective-permute-start.1 = (f32[64,2048]{1,0:T(8,128)S(1)}, f32[64,2048]{1,0:T(8,128)S(1)}, u32[]{:S(2)}, u32[]{:S(2)}) collective-permute-start(f32[64,2048]{1,0:T(8,128)S(1)} %get-tuple-element.18.field_ref.start_ref), channel_id=1, source_target_pairs={{0,12},{1,13},{2,14},{3,15},{4,4},{5,5},{6,6},{7,7},{8,8},{9,9},{1... | collective-permute-start | bytes 1572872 | tf_op jit(solution)/shard_map/ppermute | solution.py:201
  10.7 0.0 collective-permute-done.flipped_ref
  10.8 0.2 collective-permute-start.5
  11.0 1.9 %collective-permute-start.2 = (f32[32,2048]{1,0:T(8,128)S(1)}, f32[32,2048]{1,0:T(8,128)S(1)}, u32[]{:S(2)}, u32[]{:S(2)}) collective-permute-start(f32[32,2048]{1,0:T(8,128)S(1)} %get-tuple-element.19), channel_id=1, source_target_pairs={{0,6},{1,7},{2,2},{3,3},{4,4},{5,5},{6,0},{7,1},{8,14},{9,15},{10,... | collective-permute-start | bytes 786440 | tf_op jit(solution)/shard_map/ppermute | solution.py:201
  12.9 0.7 collective-permute-done.3
  13.6 1.3 %collective-permute-start.4 = (f32[32,2048]{1,0:T(8,128)S(1)}, f32[32,2048]{1,0:T(8,128)S(1)}, u32[]{:S(2)}, u32[]{:S(2)}) collective-permute-start(f32[32,2048]{1,0:T(8,128)S(1)} %collective-permute-done.3), channel_id=1, source_target_pairs={{2,6},{3,7},{4,0},{5,1},{10,14},{11,15},{12,8},{13,9},{18,22},{19,... | collective-permute-start | bytes 786440 | tf_op jit(solution)/shard_map/ppermute | solution.py:263
  14.8 0.1 pad_add_fusion.place_ref
  14.9 2.2 %copy-done = f32[64,128,128]{2,1,0:T(8,128)S(1)} copy-done((f32[64,128,128]{2,1,0:T(8,128)S(1)}, f32[64,128,128]{2,1,0:T(8,128)}, u32[]{:S(2)}) %copy-start) | copy-done | bytes 4194328
  17.1 0.7 copy-done.3
  17.8 0.7 copy-done.4
  18.5 0.7 copy-done.5
  19.1 3.6 %own.2.own_ref = f32[64,2048]{1,0:T(8,128)S(1)} custom-call(s32[2]{0:T(128)S(1)} %pad_add_fusion.place_ref, s32[64]{0:T(128)S(1)} %copy-done.4, s32[4]{0:T(128)S(1)} %copy-done.5, f32[64,2048]{1,0:T(8,128)S(1)} %get-tuple-element.18.field_ref.start_ref, f32[64,2048]{1,0:T(8,128)S(1)} %collective-permute-done.flipped_ref, f32[16,4,128,128]{3,2,1,0:T(8,128)S(1)} %bitcast.4, ...), custom_call_target="tpu_custom_call" | custom-call | flops 536870912 | bytes 5767168 | tf_op jit(solution)/shard_map/own/pallas_call | solution.py:233
  22.7 7.9 %collective-permute-done.2.refs_1_ = f32[32,2048]{1,0:T(8,128)S(1)} collective-permute-done((f32[32,2048]{1,0:T(8,128)S(1)}, f32[32,2048]{1,0:T(8,128)S(1)}, u32[]{:S(2)}, u32[]{:S(2)}) %collective-permute-start.2) | collective-permute-done | bytes 262176 | tf_op jit(solution)/shard_map/ppermute | solution.py:201
  30.6 0.0 collective-permute-done.4.refs_2_
  30.7 0.7 combine.1
  31.4 0.2 collective-permute-start.6
  31.6 1.9 %collective-permute-start.7 = (f32[64,2048]{1,0:T(8,128)S(1)}, f32[64,2048]{1,0:T(8,128)S(1)}, u32[]{:S(2)}, u32[]{:S(2)}) collective-permute-start(f32[64,2048]{1,0:T(8,128)S(1)} %get-tuple-element.21.field_ref), channel_id=1, source_target_pairs={{0,12},{1,13},{2,14},{3,15},{4,4},{5,5},{6,6},{7,7},{8,8},{9,9},{1... | collective-permute-start | bytes 1572872 | tf_op jit(solution)/shard_map/ppermute | solution.py:201
  33.5 6.0 %collective-permute-start.9 = (f32[32,2048]{1,0:T(8,128)S(1)}, f32[32,2048]{1,0:T(8,128)S(1)}, u32[]{:S(2)}, u32[]{:S(2)}) collective-permute-start(f32[32,2048]{1,0:T(8,128)S(1)} %get-tuple-element.23), channel_id=1, source_target_pairs={{0,2},{1,3},{6,4},{7,5},{8,10},{9,11},{14,12},{15,13},{16,18},{17,... | collective-permute-start | bytes 786440 | tf_op jit(solution)/shard_map/ppermute | solution.py:263
  39.5 0.0 collective-permute-done.6.flipped_ref
  39.5 0.0 collective-permute-start.11
  39.5 1.9 %collective-permute-start.8 = (f32[32,2048]{1,0:T(8,128)S(1)}, f32[32,2048]{1,0:T(8,128)S(1)}, u32[]{:S(2)}, u32[]{:S(2)}) collective-permute-start(f32[32,2048]{1,0:T(8,128)S(1)} %get-tuple-element.22), channel_id=1, source_target_pairs={{0,6},{1,7},{2,2},{3,3},{4,4},{5,5},{6,0},{7,1},{8,14},{9,15},{10,... | collective-permute-start | bytes 786440 | tf_op jit(solution)/shard_map/ppermute | solution.py:201
  41.4 4.7 %collective-permute-done.9 = f32[32,2048]{1,0:T(8,128)S(1)} collective-permute-done((f32[32,2048]{1,0:T(8,128)S(1)}, f32[32,2048]{1,0:T(8,128)S(1)}, u32[]{:S(2)}, u32[]{:S(2)}) %collective-permute-start.9) | collective-permute-done | bytes 262176 | tf_op jit(solution)/shard_map/ppermute | solution.py:263
  46.1 1.3 %collective-permute-start.10 = (f32[32,2048]{1,0:T(8,128)S(1)}, f32[32,2048]{1,0:T(8,128)S(1)}, u32[]{:S(2)}, u32[]{:S(2)}) collective-permute-start(f32[32,2048]{1,0:T(8,128)S(1)} %collective-permute-done.9), channel_id=1, source_target_pairs={{2,6},{3,7},{4,0},{5,1},{10,14},{11,15},{12,8},{13,9},{18,22},{19,... | collective-permute-start | bytes 786440 | tf_op jit(solution)/shard_map/ppermute | solution.py:263
  47.4 3.6 %own.3.own_ref = f32[64,2048]{1,0:T(8,128)S(1)} custom-call(s32[2]{0:T(128)S(1)} %pad_add_fusion.place_ref, s32[64]{0:T(128)S(1)} %copy-done.4, s32[4]{0:T(128)S(1)} %copy-done.5, f32[64,2048]{1,0:T(8,128)S(1)} %get-tuple-element.21.field_ref, f32[64,2048]{1,0:T(8,128)S(1)} %collective-permute-done.6.flipped_ref, f32[16,4,128,128]{3,2,1,0:T(8,128)S(1)} %bitcast.5, ...), custom_call_target="tpu_custom_call" | custom-call | flops 536870912 | bytes 5767168 | tf_op jit(solution)/shard_map/own/pallas_call | solution.py:233
  51.0 4.1 %collective-permute-done.8.refs_1_ = f32[32,2048]{1,0:T(8,128)S(1)} collective-permute-done((f32[32,2048]{1,0:T(8,128)S(1)}, f32[32,2048]{1,0:T(8,128)S(1)}, u32[]{:S(2)}, u32[]{:S(2)}) %collective-permute-start.8) | collective-permute-done | bytes 262176 | tf_op jit(solution)/shard_map/ppermute | solution.py:201
  55.1 0.1 collective-permute-done.10.refs_2_
  55.2 0.0 collective-permute-done.11.refs_3_
  55.2 0.8 filter.1
  56.0 0.1 collective-permute-start.12
  56.1 1.3 %collective-permute-start.13 = (f32[64,1536]{1,0:T(8,128)S(1)}, f32[64,1536]{1,0:T(8,128)S(1)}, u32[]{:S(2)}, u32[]{:S(2)}) collective-permute-start(f32[64,1536]{1,0:T(8,128)S(1)} %get-tuple-element.30), channel_id=1, source_target_pairs={{2,14},{3,15},{12,0},{13,1},{18,30},{19,31},{28,16},{29,17}} | collective-permute-start | bytes 1179656 | tf_op jit(solution)/shard_map/ppermute | solution.py:209
  57.4 0.6 collective-permute-done.12.flipped_ref
  58.0 3.5 %collective-permute-start.16 = (f32[64,1024]{1,0:T(8,128)S(1)}, f32[64,1024]{1,0:T(8,128)S(1)}, u32[]{:S(2)}, u32[]{:S(2)}) collective-permute-start(f32[64,1024]{1,0:T(8,128)S(1)} %get-tuple-element.32), channel_id=1, source_target_pairs={{0,6},{1,7},{2,2},{3,3},{4,4},{5,5},{6,0},{7,1},{8,14},{9,15},{10,... | collective-permute-start | bytes 786440 | tf_op jit(solution)/shard_map/ppermute | solution.py:201
  61.5 2.9 %collective-permute-start.15 = (f32[64,1024]{1,0:T(8,128)S(1)}, f32[64,1024]{1,0:T(8,128)S(1)}, u32[]{:S(2)}, u32[]{:S(2)}) collective-permute-start(f32[64,1024]{1,0:T(8,128)S(1)} %get-tuple-element.32), channel_id=1, source_target_pairs={{0,3},{1,1},{2,2},{3,0},{4,7},{5,5},{6,6},{7,4},{8,11},{9,9},{10,1... | collective-permute-start | bytes 786440 | tf_op jit(solution)/shard_map/ppermute | solution.py:201
  64.4 3.0 %collective-permute-start.14 = (f32[64,512]{1,0:T(8,128)S(1)}, f32[64,512]{1,0:T(8,128)S(1)}, u32[]{:S(2)}, u32[]{:S(2)}) collective-permute-start(f32[64,512]{1,0:T(8,128)S(1)} %get-tuple-element.31), channel_id=1, source_target_pairs={{0,12},{1,13},{14,2},{15,3},{16,28},{17,29},{30,18},{31,19}} | collective-permute-start | bytes 393224 | tf_op jit(solution)/shard_map/ppermute | solution.py:209
  67.5 5.7 %own_gram.1 = (f32[64,128]{1,0:T(8,128)S(1)}, f32[64,2048]{1,0:T(8,128)}) custom-call(s32[2]{0:T(128)S(1)} %pad_add_fusion.place_ref, s32[64]{0:T(128)S(1)} %copy-done.4, s32[4]{0:T(128)S(1)} %copy-done.5, s32[1]{0:T(128)S(6)} %copy.9.live_ref, f32[64,2048]{1,0:T(8,128)S(1)} %get-tuple-element.24.field_ref, ...), custom_call_target="tpu_custom_call" | custom-call | flops 536870912 | bytes 5767168 | tf_op jit(solution)/shard_map/own_gram/pallas_call | solution.py:245
  73.2 0.0 collective-permute-done.13.refs_0_
  73.2 1.2 %crossed.1 = f32[64,128]{1,0:T(8,128)S(1)} custom-call(s32[2]{0:T(128)S(1)} %pad_add_fusion.place_ref, f32[64,128]{1,0:T(8,128)S(1)} %get-tuple-element.29.own_ref, f32[64,2048]{1,0:T(8,128)S(1)} %get-tuple-element.24.field_ref, f32[64,1536]{1,0:T(8,128)S(1)} %collective-permute-done.13.refs_0_, f32[64,512]{1,0:T(8,128)S(1)} %collective-permute-done.14.refs_1_, ...), custom_call_target="tpu_custom_call" | custom-call | tf_op jit(solution)/shard_map/crossed/pallas_call | solution.py:301
  74.4 0.1 collective-permute-start.17
  74.5 1.2 %collective-permute-done.17 = f32[64,128]{1,0:T(8,128)S(1)} collective-permute-done((f32[64,128]{1,0:T(8,128)S(1)}, f32[64,128]{1,0:T(8,128)S(1)}, u32[]{:S(2)}, u32[]{:S(2)}) %collective-permute-start.17) | collective-permute-done | bytes 32800 | tf_op jit(solution)/shard_map/ppermute | solution.py:216
  75.7 3.9 %collective-permute-done.18 = f32[64,128]{1,0:T(8,128)S(1)} collective-permute-done((f32[64,128]{1,0:T(8,128)S(1)}, f32[64,128]{1,0:T(8,128)S(1)}, u32[]{:S(2)}, u32[]{:S(2)}) %collective-permute-start.18) | collective-permute-done | bytes 32800 | tf_op jit(solution)/shard_map/ppermute | solution.py:216
  79.6 3.9 %collective-permute-done.19 = f32[64,128]{1,0:T(8,128)S(1)} collective-permute-done((f32[64,128]{1,0:T(8,128)S(1)}, f32[64,128]{1,0:T(8,128)S(1)}, u32[]{:S(2)}, u32[]{:S(2)}) %collective-permute-start.19) | collective-permute-done | bytes 32800 | tf_op jit(solution)/shard_map/ppermute | solution.py:216
  83.5 0.1 collective-permute-start.20
  83.6 4.8 %collective-permute-done.20 = f32[64,128]{1,0:T(8,128)S(1)} collective-permute-done((f32[64,128]{1,0:T(8,128)S(1)}, f32[64,128]{1,0:T(8,128)S(1)}, u32[]{:S(2)}, u32[]{:S(2)}) %collective-permute-start.20) | collective-permute-done | bytes 32800 | tf_op jit(solution)/shard_map/ppermute | solution.py:216
  88.4 0.7 fusion
  (19 shorter events, 0.1 us)
Async XLA Ops:
  1.3 1.0 %copy-start.2 = (f32[64,2048]{1,0:T(8,128)S(1)}, f32[64,2048]{1,0:T(8,128)}, u32[]{:S(2)}) copy-start(f32[64,2048]{1,0:T(8,128)} %vectors_ref.1) | copy-start | bytes 1572868
  2.4 8.3 %collective-permute-start = (f32[64,2048]{1,0:T(8,128)S(1)}, f32[64,2048]{1,0:T(8,128)S(1)}, u32[]{:S(2)}, u32[]{:S(2)}) collective-permute-start(f32[64,2048]{1,0:T(8,128)S(1)} %get-tuple-element.18.field_ref.start_ref), channel_id=1, source_target_pairs={{0,1},{1,0},{2,3},{3,2},{4,5},{5,4},{6,7},{7,6},{8,9},{9,8},{10,11... | collective-permute-start | bytes 1572872 | tf_op jit(solution)/shard_map/ppermute | solution.py:216
  2.9 10.6 %collective-permute-start.3 = (f32[32,2048]{1,0:T(8,128)S(1)}, f32[32,2048]{1,0:T(8,128)S(1)}, u32[]{:S(2)}, u32[]{:S(2)}) collective-permute-start(f32[32,2048]{1,0:T(8,128)S(1)} %get-tuple-element.20), channel_id=1, source_target_pairs={{0,2},{1,3},{6,4},{7,5},{8,10},{9,11},{14,12},{15,13},{16,18},{17,... | collective-permute-start | bytes 786440 | tf_op jit(solution)/shard_map/ppermute | solution.py:263
  7.4 23.3 %collective-permute-start.1 = (f32[64,2048]{1,0:T(8,128)S(1)}, f32[64,2048]{1,0:T(8,128)S(1)}, u32[]{:S(2)}, u32[]{:S(2)}) collective-permute-start(f32[64,2048]{1,0:T(8,128)S(1)} %get-tuple-element.18.field_ref.start_ref), channel_id=1, source_target_pairs={{0,12},{1,13},{2,14},{3,15},{4,4},{5,5},{6,6},{7,7},{8,8},{9,9},{1... | collective-permute-start | bytes 1572872 | tf_op jit(solution)/shard_map/ppermute | solution.py:201
  10.8 19.9 %collective-permute-start.5 = (f32[64,2048]{1,0:T(8,128)S(1)}, f32[64,2048]{1,0:T(8,128)S(1)}, u32[]{:S(2)}, u32[]{:S(2)}) collective-permute-start(f32[64,2048]{1,0:T(8,128)S(1)} %collective-permute-done.flipped_ref), channel_id=1, source_target_pairs={{0,1},{1,3},{2,0},{3,2},{4,5},{5,7},{6,4},{7,6},{8,9},{9,11},{10,8... | collective-permute-start | bytes 1572872 | tf_op jit(solution)/shard_map/ppermute | solution.py:213
  11.0 19.7 %collective-permute-start.2 = (f32[32,2048]{1,0:T(8,128)S(1)}, f32[32,2048]{1,0:T(8,128)S(1)}, u32[]{:S(2)}, u32[]{:S(2)}) collective-permute-start(f32[32,2048]{1,0:T(8,128)S(1)} %get-tuple-element.19), channel_id=1, source_target_pairs={{0,6},{1,7},{2,2},{3,3},{4,4},{5,5},{6,0},{7,1},{8,14},{9,15},{10,... | collective-permute-start | bytes 786440 | tf_op jit(solution)/shard_map/ppermute | solution.py:201
  13.6 17.1 %collective-permute-start.4 = (f32[32,2048]{1,0:T(8,128)S(1)}, f32[32,2048]{1,0:T(8,128)S(1)}, u32[]{:S(2)}, u32[]{:S(2)}) collective-permute-start(f32[32,2048]{1,0:T(8,128)S(1)} %collective-permute-done.3), channel_id=1, source_target_pairs={{2,6},{3,7},{4,0},{5,1},{10,14},{11,15},{12,8},{13,9},{18,22},{19,... | collective-permute-start | bytes 786440 | tf_op jit(solution)/shard_map/ppermute | solution.py:263
  14.9 2.2 %copy-start = (f32[64,128,128]{2,1,0:T(8,128)S(1)}, f32[64,128,128]{2,1,0:T(8,128)}, u32[]{:S(2)}) copy-start(f32[64,128,128]{2,1,0:T(8,128)} %param.7) | copy-start | bytes 12582916
  17.1 0.7 copy-start.3
  17.8 0.7 copy-start.4
  18.5 0.7 copy-start.5
  19.1 28.3 %copy-start.1 = (f32[64,128,128]{2,1,0:T(8,128)S(1)}, f32[64,128,128]{2,1,0:T(8,128)}, u32[]{:S(2)}) copy-start(f32[64,128,128]{2,1,0:T(8,128)} %param.7) | copy-start | bytes 12582916
  31.4 8.1 %collective-permute-start.6 = (f32[64,2048]{1,0:T(8,128)S(1)}, f32[64,2048]{1,0:T(8,128)S(1)}, u32[]{:S(2)}, u32[]{:S(2)}) collective-permute-start(f32[64,2048]{1,0:T(8,128)S(1)} %get-tuple-element.21.field_ref), channel_id=1, source_target_pairs={{0,1},{1,0},{2,3},{3,2},{4,5},{5,4},{6,7},{7,6},{8,9},{9,8},{10,11... | collective-permute-start | bytes 1572872 | tf_op jit(solution)/shard_map/ppermute | solution.py:216
  31.6 23.6 %collective-permute-start.7 = (f32[64,2048]{1,0:T(8,128)S(1)}, f32[64,2048]{1,0:T(8,128)S(1)}, u32[]{:S(2)}, u32[]{:S(2)}) collective-permute-start(f32[64,2048]{1,0:T(8,128)S(1)} %get-tuple-element.21.field_ref), channel_id=1, source_target_pairs={{0,12},{1,13},{2,14},{3,15},{4,4},{5,5},{6,6},{7,7},{8,8},{9,9},{1... | collective-permute-start | bytes 1572872 | tf_op jit(solution)/shard_map/ppermute | solution.py:201
  33.5 12.6 %collective-permute-start.9 = (f32[32,2048]{1,0:T(8,128)S(1)}, f32[32,2048]{1,0:T(8,128)S(1)}, u32[]{:S(2)}, u32[]{:S(2)}) collective-permute-start(f32[32,2048]{1,0:T(8,128)S(1)} %get-tuple-element.23), channel_id=1, source_target_pairs={{0,2},{1,3},{6,4},{7,5},{8,10},{9,11},{14,12},{15,13},{16,18},{17,... | collective-permute-start | bytes 786440 | tf_op jit(solution)/shard_map/ppermute | solution.py:263
  39.5 15.8 %collective-permute-start.11 = (f32[64,2048]{1,0:T(8,128)S(1)}, f32[64,2048]{1,0:T(8,128)S(1)}, u32[]{:S(2)}, u32[]{:S(2)}) collective-permute-start(f32[64,2048]{1,0:T(8,128)S(1)} %collective-permute-done.6.flipped_ref), channel_id=1, source_target_pairs={{0,1},{1,3},{2,0},{3,2},{4,5},{5,7},{6,4},{7,6},{8,9},{9,11},{10,8... | collective-permute-start | bytes 1572872 | tf_op jit(solution)/shard_map/ppermute | solution.py:213
  39.5 15.6 %collective-permute-start.8 = (f32[32,2048]{1,0:T(8,128)S(1)}, f32[32,2048]{1,0:T(8,128)S(1)}, u32[]{:S(2)}, u32[]{:S(2)}) collective-permute-start(f32[32,2048]{1,0:T(8,128)S(1)} %get-tuple-element.22), channel_id=1, source_target_pairs={{0,6},{1,7},{2,2},{3,3},{4,4},{5,5},{6,0},{7,1},{8,14},{9,15},{10,... | collective-permute-start | bytes 786440 | tf_op jit(solution)/shard_map/ppermute | solution.py:201
  46.1 9.1 %collective-permute-start.10 = (f32[32,2048]{1,0:T(8,128)S(1)}, f32[32,2048]{1,0:T(8,128)S(1)}, u32[]{:S(2)}, u32[]{:S(2)}) collective-permute-start(f32[32,2048]{1,0:T(8,128)S(1)} %collective-permute-done.9), channel_id=1, source_target_pairs={{2,6},{3,7},{4,0},{5,1},{10,14},{11,15},{12,8},{13,9},{18,22},{19,... | collective-permute-start | bytes 786440 | tf_op jit(solution)/shard_map/ppermute | solution.py:263
  56.0 2.0 %collective-permute-start.12 = (f32[64,2048]{1,0:T(8,128)S(1)}, f32[64,2048]{1,0:T(8,128)S(1)}, u32[]{:S(2)}, u32[]{:S(2)}) collective-permute-start(f32[64,2048]{1,0:T(8,128)S(1)} %get-tuple-element.24.field_ref), channel_id=1, source_target_pairs={{0,1},{1,0},{2,3},{3,2},{4,5},{5,4},{6,7},{7,6},{8,9},{9,8},{10,11... | collective-permute-start | bytes 1572872 | tf_op jit(solution)/shard_map/ppermute | solution.py:216
  56.1 17.1 %collective-permute-start.13 = (f32[64,1536]{1,0:T(8,128)S(1)}, f32[64,1536]{1,0:T(8,128)S(1)}, u32[]{:S(2)}, u32[]{:S(2)}) collective-permute-start(f32[64,1536]{1,0:T(8,128)S(1)} %get-tuple-element.30), channel_id=1, source_target_pairs={{2,14},{3,15},{12,0},{13,1},{18,30},{19,31},{28,16},{29,17}} | collective-permute-start | bytes 1179656 | tf_op jit(solution)/shard_map/ppermute | solution.py:209
  58.0 15.2 %collective-permute-start.16 = (f32[64,1024]{1,0:T(8,128)S(1)}, f32[64,1024]{1,0:T(8,128)S(1)}, u32[]{:S(2)}, u32[]{:S(2)}) collective-permute-start(f32[64,1024]{1,0:T(8,128)S(1)} %get-tuple-element.32), channel_id=1, source_target_pairs={{0,6},{1,7},{2,2},{3,3},{4,4},{5,5},{6,0},{7,1},{8,14},{9,15},{10,... | collective-permute-start | bytes 786440 | tf_op jit(solution)/shard_map/ppermute | solution.py:201
  61.5 11.7 %collective-permute-start.15 = (f32[64,1024]{1,0:T(8,128)S(1)}, f32[64,1024]{1,0:T(8,128)S(1)}, u32[]{:S(2)}, u32[]{:S(2)}) collective-permute-start(f32[64,1024]{1,0:T(8,128)S(1)} %get-tuple-element.32), channel_id=1, source_target_pairs={{0,3},{1,1},{2,2},{3,0},{4,7},{5,5},{6,6},{7,4},{8,11},{9,9},{10,1... | collective-permute-start | bytes 786440 | tf_op jit(solution)/shard_map/ppermute | solution.py:201
  64.4 8.8 %collective-permute-start.14 = (f32[64,512]{1,0:T(8,128)S(1)}, f32[64,512]{1,0:T(8,128)S(1)}, u32[]{:S(2)}, u32[]{:S(2)}) collective-permute-start(f32[64,512]{1,0:T(8,128)S(1)} %get-tuple-element.31), channel_id=1, source_target_pairs={{0,12},{1,13},{14,2},{15,3},{16,28},{17,29},{30,18},{31,19}} | collective-permute-start | bytes 393224 | tf_op jit(solution)/shard_map/ppermute | solution.py:209
  74.4 1.3 %collective-permute-start.17 = (f32[64,128]{1,0:T(8,128)S(1)}, f32[64,128]{1,0:T(8,128)S(1)}, u32[]{:S(2)}, u32[]{:S(2)}) collective-permute-start(f32[64,128]{1,0:T(8,128)S(1)} %crossed.1), channel_id=1, source_target_pairs={{0,1},{1,0},{2,3},{3,2},{4,5},{5,4},{6,7},{7,6},{8,9},{9,8},{10,11... | collective-permute-start | bytes 98312 | tf_op jit(solution)/shard_map/ppermute | solution.py:216
  75.7 3.9 %collective-permute-start.18 = (f32[64,128]{1,0:T(8,128)S(1)}, f32[64,128]{1,0:T(8,128)S(1)}, u32[]{:S(2)}, u32[]{:S(2)}) collective-permute-start(f32[64,128]{1,0:T(8,128)S(1)} %add.20), channel_id=1, source_target_pairs={{0,2},{1,3},{2,0},{3,1},{4,6},{5,7},{6,4},{7,5},{8,10},{9,11},{10,... | collective-permute-start | bytes 98312 | tf_op jit(solution)/shard_map/ppermute | solution.py:216
  79.6 3.9 %collective-permute-start.19 = (f32[64,128]{1,0:T(8,128)S(1)}, f32[64,128]{1,0:T(8,128)S(1)}, u32[]{:S(2)}, u32[]{:S(2)}) collective-permute-start(f32[64,128]{1,0:T(8,128)S(1)} %add.21), channel_id=1, source_target_pairs={{0,4},{1,5},{2,6},{3,7},{4,0},{5,1},{6,2},{7,3},{8,12},{9,13},{10,... | collective-permute-start | bytes 98312 | tf_op jit(solution)/shard_map/ppermute | solution.py:216
  83.5 4.8 %collective-permute-start.20 = (f32[64,128]{1,0:T(8,128)S(1)}, f32[64,128]{1,0:T(8,128)S(1)}, u32[]{:S(2)}, u32[]{:S(2)}) collective-permute-start(f32[64,128]{1,0:T(8,128)S(1)} %add.22), channel_id=1, source_target_pairs={{0,8},{1,9},{2,10},{3,11},{4,12},{5,13},{6,14},{7,15},{8,0},{9,1},... | collective-permute-start | bytes 98312 | tf_op jit(solution)/shard_map/ppermute | solution.py:216
